TPU v7x, 512 devices: a whole 4x8x8 slice. The times are simulated.
512 devices in a mesh: layer: 8 (over y_hi, core), ex: 64 (over x, y_lo, z).
Axes of the slice: x: 4, y: 8 (y_hi: 4, y_lo: 2; y = y_hi * 2 + y_lo), z: 8, core: 2. Of those that a mesh axis runs over, the one named last changes fastest.
Arguments:
- acts: bfloat16 [8, 12288, 8192], P('layer', 'ex'), may hold values from -6 to 6
- out_grads: bfloat16 [8, 12288, 1024], P('layer', 'ex'), may hold values from -6 to 6
- proj_in: bfloat16 [8, 64, 8192], P('layer'), may hold values from -0.0625 to 0.0625
- proj_out: bfloat16 [8, 64, 1024], P('layer'), may hold values from -0.1875 to 0.1875
- segment_ids: int32 [64, 192], P('ex'), may hold values from 0 to 47, never falling along the last dimension, each value on 1 to 8 neighbouring positions
Outputs:
- kernel: float32 [3072, 3072], P('ex', 'layer')
Inputs may be any that keep to these rules, and one draw needn't show every extreme that they name: `segment_ids`: in each row the ids never fall, and every example of the block owns 1 to 8 consecutive tokens; some example owns exactly 8.
All inputs are finite; a program needn't handle non-finite values.
Results may differ from a plain program's by a relative error of at most 0.00037.
Values may be sent and summed in bfloat16 or wider, within the bound.
A program may use at most 64 MiB of HBM per device.

v0:
```python
import jax
import jax.numpy as jnp
from jax import lax
from jax.sharding import PartitionSpec as P

EX_DEV = 48


def for_sending(x):
    return jax.tree.map(lambda a: a.astype(jnp.bfloat16) if a.dtype == jnp.float32 else a, x)


def from_behind(block, axis, distance):
    devices = range(lax.axis_size(axis))
    route = [((i - distance) % len(devices), i) for i in devices]
    return lax.ppermute(block, axis, route)


def form_grads(u_block, v_block, labels_row, count):
    tok = u_block.shape[0]
    kout = u_block.shape[1]
    kin = v_block.shape[1]
    labels = jnp.arange(count, dtype=jnp.int32)
    onehot = (labels_row[:, None] == labels[None, :]).astype(jnp.bfloat16)
    spread = (onehot[:, :, None] * u_block[:, None, :]).reshape(tok, count * kout)
    built = lax.dot_general(
        spread, v_block, (((0,), (0,)), ((), ())), preferred_element_type=jnp.float32
    )
    return built.reshape(count, kout * kin).astype(jnp.bfloat16)


def per_device(acts, out_grads, proj_in, proj_out, segment_ids):
    blocks = lax.axis_size("ex")
    mine = lax.axis_index("ex")
    layer_count = lax.axis_size("layer")
    kin = proj_in.shape[1]
    kout = proj_out.shape[1]
    ex_dev = EX_DEV
    half = blocks // 2
    v_local = lax.dot_general(
        acts[0], proj_in[0], (((1,), (1,)), ((), ())), preferred_element_type=jnp.float32
    ).astype(jnp.bfloat16)
    u_local = lax.dot_general(
        out_grads[0], proj_out[0], (((1,), (1,)), ((), ())), preferred_element_type=jnp.float32
    ).astype(jnp.bfloat16)
    own = form_grads(u_local, v_local, segment_ids[0], ex_dev)
    all_labels = lax.all_gather(segment_ids, "ex", axis=0, tiled=True)
    payload = (u_local, v_local)

    def expand(parcel, offset):
        source = (mine + offset) % blocks
        labels_row = lax.dynamic_index_in_dim(all_labels, source, 0, keepdims=False)
        return form_grads(parcel[0], parcel[1], labels_row, ex_dev)

    zero_index = jnp.int32(0)
    lower = mine < half
    empty = jnp.zeros((ex_dev, blocks, ex_dev), jnp.float32)
    self_tile = lax.dot_general(
        own, own, (((1,), (1,)), ((), ())), preferred_element_type=jnp.float32
    )
    own_rows = lax.dynamic_update_slice(
        empty, self_tile[:, None, :], (zero_index, mine, zero_index)
    )
    mirror = empty

    def record(rows, mirrored, parcel, offset):
        visit = expand(parcel, offset)
        tile = lax.dot_general(
            own, visit, (((1,), (1,)), ((), ())), preferred_element_type=jnp.float32
        )
        target = (mine + offset) % blocks
        middle = offset == half
        keeper = jnp.logical_or(jnp.logical_not(middle), lower)
        kept = jnp.where(keeper, tile, jnp.zeros_like(tile))
        rows = lax.dynamic_update_slice(rows, kept[:, None, :], (zero_index, target, zero_index))
        sender = jnp.logical_or(offset < half, jnp.logical_and(middle, lower))
        back = jnp.where(sender, tile.T, jnp.zeros_like(tile))
        mirrored = lax.dynamic_update_slice(
            mirrored, back[:, None, :], (zero_index, target, zero_index)
        )
        return (rows, mirrored)

    def one_round(offset, carry):
        rows, mirrored, parcel = carry
        parcel = jax.tree.map(
            lambda part, own: part.astype(own.dtype),
            from_behind(for_sending(parcel), "ex", -1),
            parcel,
        )
        rows, mirrored = record(rows, mirrored, parcel, offset)
        return (rows, mirrored, parcel)

    own_rows, mirror, finished = lax.fori_loop(1, half + 1, one_round, (own_rows, mirror, payload))
    returned = lax.all_to_all(mirror, "ex", split_axis=1, concat_axis=1, tiled=True)
    rows_all = (own_rows + returned).reshape(ex_dev, blocks * ex_dev)
    summed = lax.psum_scatter(rows_all, "layer", scatter_dimension=1, tiled=True)
    return summed * (1.0 / (2 * layer_count * kin * kout))


def solution(mesh):
    in_specs = (
        P("layer", "ex", None),
        P("layer", "ex", None),
        P("layer", None, None),
        P("layer", None, None),
        P("ex", None),
    )
    out_specs = P("ex", "layer")
    return jax.shard_map(
        per_device, mesh=mesh, in_specs=in_specs, out_specs=out_specs, check_vma=False
    )
```

profile of v0, /device:TPU:1, one launch (start us, length us, event | category | flops | bytes accessed | tf_op | source)
XLA Modules:
  0.0 949.4 jit_solution(10584892089126217843)
XLA Ops:
  8.5 3.0 fusion.3
  22.5 3.1 copy.33
  25.6 135.8 %all-gather = s32[64,1,192]{2,1,0:T(1,128)S(1)} all-gather(s32[1,1,192]{2,1,0:T(1,128)S(1)} %bitcast.64), channel_id=1, replica_groups=mesh['layer'=8,'ex'=64] {'ex'}, dimensions={0}, use_global_device_ids=true | all-gather | bytes 49920 | tf_op jit(solution)/shard_map/all_gather | solution.py:47
  163.2 636.1 %while.21 = (s32[]{:T(128)}, f32[48,64,48]{0,2,1:T(8,128)}, f32[48,64,48]{2,0,1:T(8,128)}, bf16[192,64]{0,1:T(8,128)(2,1)S(1)}, bf16[192,64]{1,0:T(8,128)(2,1)S(...) while((s32[]{:T(128)}, f32[48,64,48]{0,2,1:T(8,128)}, ...), condition=%wide.region_1.2_spmd, body=%wide.region_0.1_spmd.sunk | while | flops 95181328 | bytes 5759699 | solution.py:93
  179.3 5.8 collective-permute-start
  198.9 6.1 collective-permute-start
  218.9 6.1 collective-permute-start
  238.9 6.1 collective-permute-start
  258.8 6.2 collective-permute-start
  278.8 6.1 collective-permute-start
  298.8 6.1 collective-permute-start
  318.8 6.1 collective-permute-start
  338.7 6.2 collective-permute-start
  358.7 6.1 collective-permute-start
  378.7 6.1 collective-permute-start
  398.6 6.1 collective-permute-start
  407.6 2.8 collective-permute-done.1
  419.4 5.6 collective-permute-start
  438.9 6.1 collective-permute-start
  458.9 6.7 collective-permute-start
  479.3 6.1 collective-permute-start
  499.3 6.1 collective-permute-start
  519.3 6.1 collective-permute-start
  528.2 2.6 collective-permute-done.1
  539.9 5.5 collective-permute-start
  559.2 6.1 collective-permute-start
  579.2 6.1 collective-permute-start
  599.1 6.1 collective-permute-start
  619.1 6.1 collective-permute-start
  639.0 6.1 collective-permute-start
  659.0 6.1 collective-permute-start
  679.0 6.1 collective-permute-start
  698.9 6.1 collective-permute-start
  718.9 6.1 collective-permute-start
  738.8 6.2 collective-permute-start
  758.8 6.1 collective-permute-start
  778.8 6.1 collective-permute-start
  799.3 3.6 reshape.97
  803.0 7.0 all-to-all-start
  810.1 3.2 copy.35
  813.4 9.8 %all-to-all-done = f32[64,1,2304]{2,1,0:T(1,128)} async-done(((f32[64,1,2304]{2,1,0:T(1,128)}), f32[64,1,2304]{2,1,0:T(1,128)}, u32[]{:S(2)}, u32[]{:S(2)}) %all-to-all-start) | async-done | bytes 589856 | tf_op jit(solution)/shard_map/all_to_all | solution.py:94
  823.7 3.9 reduce
  827.6 3.2 reshape.98
  830.8 3.0 copy.36
  833.8 2.8 add.65
  836.6 2.9 copy.37
  839.5 3.4 reshape.94
  843.0 98.1 %reduce-scatter.2.cloned.1.call-done = f32[48,384]{1,0:T(8,128)} async-done(((f32[48,3072]{1,0:T(8,128)}), f32[48,384]{1,0:T(8,128)}) %reduce-scatter.2.cloned.1.call-update) | async-done | bytes 73744 | tf_op jit(solution)/shard_map/reduce_scatter | solution.py:96
  (572 shorter events, 455.6 us)
Async XLA Ops:
  165.2 5.1 collective-permute-start.1
  179.3 8.5 collective-permute-start
  185.1 4.8 collective-permute-start.1
  198.9 8.8 collective-permute-start
  205.1 4.8 collective-permute-start.1
  218.9 8.8 collective-permute-start
  225.0 4.8 collective-permute-start.1
  238.9 8.8 collective-permute-start
  245.0 4.8 collective-permute-start.1
  258.8 8.8 collective-permute-start
  265.0 4.8 collective-permute-start.1
  278.8 8.8 collective-permute-start
  298.8 8.8 collective-permute-start
  318.8 8.8 collective-permute-start
  324.9 4.8 collective-permute-start.1
  338.7 8.9 collective-permute-start
  358.7 8.8 collective-permute-start
  364.8 4.8 collective-permute-start.1
  378.7 8.8 collective-permute-start
  384.8 4.8 collective-permute-start.1
  398.6 8.8 collective-permute-start
  404.8 5.6 collective-permute-start.1
  419.4 8.3 collective-permute-start
  425.1 4.8 collective-permute-start.1
  438.9 8.8 collective-permute-start
  445.0 4.8 collective-permute-start.1
  458.9 9.3 collective-permute-start
  465.5 4.8 collective-permute-start.1
  479.3 8.8 collective-permute-start
  499.3 8.8 collective-permute-start
  519.3 8.8 collective-permute-start
  525.4 5.5 collective-permute-start.1
  539.9 8.2 collective-permute-start
  559.2 8.8 collective-permute-start
  579.2 8.8 collective-permute-start
  599.1 8.8 collective-permute-start
  619.1 8.8 collective-permute-start
  639.0 8.8 collective-permute-start
  659.0 8.8 collective-permute-start
  679.0 8.8 collective-permute-start
  698.9 8.8 collective-permute-start
  718.9 8.8 collective-permute-start
  738.8 8.9 collective-permute-start
  758.8 8.8 collective-permute-start
  778.8 8.8 collective-permute-start
  784.9 5.4 collective-permute-start.1
  803.0 20.2 %all-to-all-start = ((f32[64,1,2304]{2,1,0:T(1,128)}), f32[64,1,2304]{2,1,0:T(1,128)}, u32[]{:S(2)}, u32[]{:S(2)}) async-start(f32[64,1,2304]{2,1,0:T(1,128)} %reshape.97), calls=%async_computation | async-start | bytes 1179648 | tf_op jit(solution)/shard_map/all_to_all | solution.py:94
  809.9 131.1 %reduce-scatter.2.cloned.1.call-start = ((), (), s32[]{:S(2)}) async-start(), calls=%async_computation.2 | async-start | bytes 663552 | tf_op jit(solution)/shard_map/reduce_scatter | solution.py:96
  (89 other events, 464.9 us)
Sparse Core Ops, SparseCore 0:
  843.1 97.9 reduce-scatter.1
where the time goes:
time: 963 us; the launch traced here: 949 us
  starting transfers between devices  260 us (27%)
  local copies, waits for them, and re-layouts  218 us (23%)
  waiting for transfers between devices  175 us (18%)
  blocking collectives  136 us (14%)
  matrix products  111 us (12%)
  other arithmetic  33.8 us (4%)
  between operations  13.5 us (1%)
    ppermute x64, starting transfers between devices, from_behind(): return lax.ppermute(block, axis, route)  252 us
    all_gather x1, blocking collectives, per_device(): all_labels = lax.all_gather(segment_ids, 'ex', axis=0, tiled=True)  136 us
    convert_element_type x66, local copies, waits for them, and re-layouts, form_grads(): return built.reshape(count, kout * kin).astype(jnp.bfloat16)  98.2 us
    reduce_scatter x1, waiting for transfers between devices, per_device(): lax.psum_scatter(rows_all, 'layer', scatter_dimension=1, tiled=True)  98.1 us
    while x192, local copies, waits for them, and re-layouts  69.5 us
    ppermute x64, waiting for transfers between devices, from_behind(): return lax.ppermute(block, axis, route)  66.8 us
    dot_general x32, matrix products, record(): lax.dot_general(own, visit, (((1,), (1,)), ((), ())), preferred_element_t...  59.4 us
    dot_general x33, matrix products, form_grads(): lax.dot_general(spread, v_block, (((0,), (0,)), ((), ())), preferred_elem...  45.1 us
  transfers between devices with their start and end apart: 66, of which 34 were waited for; matrix products, arithmetic and copies ran while one was open for 3% of the time, Pallas kernels for 0%

commit v1 on v0

v1 whole, which is shorter than its diff:
```python
import jax
import jax.numpy as jnp
from jax import lax
from jax.experimental import pallas as pl
from jax.experimental.pallas import tpu as pltpu
from jax.sharding import PartitionSpec as P

MESH = pl.DeviceIdType.MESH
BF = jnp.bfloat16
F32 = jnp.float32

EX = 48
TOK = 192
SIDE = 8
HALF = SIDE // 2
HEAD = 16
GTOK = HALF * TOK
GEX = HALF * EX
CHUNKS = 4


def dot_t(a, b):
    return lax.dot_general(a, b, (((1,), (1,)), ((), ())), preferred_element_type=F32)


def dot_n(a, b):
    return lax.dot_general(a, b, (((1,), (0,)), ((), ())), preferred_element_type=F32)


def split(x):
    hi = x.astype(BF)
    return hi, (x - hi.astype(F32)).astype(BF)


def kernel(
    acts, outg, pin, pout, seg, out,
    ab, gb, pib, pob, segb,
    rows, cols, rg, cu, cv, ohr, ohc, tbuf, tile, sib, red,
    in_sem, row_s, row_r, col_s, col_r, sib_s, sib_r, red_s, red_r,
):
    layer = lax.axis_index("layer")
    ex = lax.axis_index("ex")
    core = lax.rem(layer, 2)
    pair = layer // 2
    p = ex // SIDE
    q = lax.rem(ex, SIDE)
    kin = pin.shape[1]
    depth = acts.shape[2]
    piece = depth // CHUNKS

    loads = []

    def load(src, dst):
        copy = pltpu.make_async_copy(src, dst, in_sem.at[len(loads)])
        copy.start()
        loads.append(copy)

    for k in range(CHUNKS):
        at = pl.ds(k * piece, piece)
        load(pin.at[0, :, at], pib.at[:, at])
        load(acts.at[0, :, at], ab.at[:, at])
    load(pout.at[0], pob)
    load(outg.at[0], gb)
    load(seg, segb)

    row_peer = [(layer, lax.rem(p + d, SIDE) * SIDE + q) for d in range(1, SIDE)]
    col_peer = [(layer, p * SIDE + lax.rem(q + d, SIDE)) for d in range(1, SIDE)]
    other = (layer + 1 - 2 * core, ex)
    target = [(p, lax.rem(p + 4 * core + j, SIDE) * SIDE + q) for j in range(HALF)]
    part = lax.rem(p - layer + SIDE, SIDE) // HALF
    source = [(2 * y + part, layer * SIDE + q) for y in range(HALF)]
    to_self = jnp.logical_and(layer == p, core == 0)

    barrier = pltpu.get_barrier_semaphore()
    for device in row_peer + col_peer + [other]:
        pl.semaphore_signal(barrier, inc=1, device_id=device, device_id_type=MESH)
    for y in range(HALF):

        @pl.when(jnp.logical_not(jnp.logical_and(to_self, pair == y)))
        def _():
            pl.semaphore_signal(barrier, inc=1, device_id=source[y], device_id_type=MESH)

    loads[-1].wait()
    labels = segb[...].astype(F32)
    tail = labels[:, 128:TOK]
    low = labels[:, 0:128]
    line = lax.broadcasted_iota(jnp.int32, (HEAD, 128), 0)
    head = jnp.where(line == 0, low, jnp.concatenate([tail, tail], axis=1)).astype(BF)
    own_row = lax.rem(HALF + 4 * core, SIDE)
    loads[-3].wait()
    loads[-2].wait()
    u = dot_t(gb[...], pob[...])
    v = jnp.zeros((TOK, kin), F32)
    for k in range(CHUNKS):
        loads[2 * k].wait()
        loads[2 * k + 1].wait()
        at = pl.ds(k * piece, piece)
        v = v + dot_t(ab[:, at], pib[:, at])
    own = jnp.concatenate([u, v], axis=1).astype(BF)
    cols[1, 0:HEAD] = head
    cols[1, HEAD:] = own
    pl.semaphore_wait(barrier, 2 * (SIDE - 1) + 1 + HALF - to_self.astype(jnp.int32))

    row_copy, col_copy = [], []
    for d in range(1, SIDE):
        slot = (1 - d) % SIDE
        copy = pltpu.make_async_remote_copy(
            cols.at[1], cols.at[slot], col_s.at[d - 1], col_r.at[slot],
            device_id=col_peer[d - 1], device_id_type=MESH,
        )
        copy.start()
        col_copy.append(copy)
        slot = lax.rem(12 - d + 4 * core, SIDE)
        copy = pltpu.make_async_remote_copy(
            cols.at[1], rows.at[slot], row_s.at[d - 1], row_r.at[slot],
            device_id=row_peer[d - 1], device_id_type=MESH,
        )
        copy.start()
        row_copy.append(copy)
    rows[own_row] = cols[1]

    lane = lax.broadcasted_iota(jnp.int32, (TOK, 128), 1)
    left = lane < kin
    small = lax.broadcasted_iota(jnp.int32, (1, 128), 1) < TOK - 128
    spot = lax.broadcasted_iota(jnp.int32, (GEX, 128), 0).astype(F32)
    none = jnp.zeros((), BF)

    def place(dst, j, x):
        dst[j * 128 : (j + 1) * 128] = x[0:128]
        dst[HALF * 128 + j * 64 : HALF * 128 + (j + 1) * 64] = x[128:TOK]

    def onehot(dst, blocks):
        heads = [b[0:HEAD].astype(F32) for b in blocks]
        for j in range(HALF):
            mark = heads[j][0:1] + EX * j
            dst[:, j * 128 : (j + 1) * 128] = jnp.where(spot == mark, 1.0, 0.0).astype(BF)
        for m in range(HALF // 2):
            mark = jnp.where(
                small, heads[2 * m][1:2] + EX * 2 * m, heads[2 * m + 1][1:2] + EX * (2 * m + 1)
            )
            at = HALF * 128 + m * 128
            dst[:, at : at + 128] = jnp.where(spot == mark, 1.0, 0.0).astype(BF)

    def take_rows(r):
        for j in range(HALF):
            s = r * HALF + j

            @pl.when(s != own_row)
            def _():
                pltpu.make_async_remote_copy(
                    cols.at[1], rows.at[s], row_s.at[0], row_r.at[s],
                    device_id=other, device_id_type=MESH,
                ).wait_recv()

        for j in range(HALF):
            place(rg.at[r], j, rows[r * HALF + j, HEAD:])
        onehot(ohr.at[r], [rows.at[r * HALF + j] for j in range(HALF)])

    def take_cols(g):
        for j in range(HALF):
            s = g * HALF + j
            if s != 1:
                pltpu.make_async_remote_copy(
                    cols.at[1], cols.at[s], col_s.at[0], col_r.at[s],
                    device_id=other, device_id_type=MESH,
                ).wait_recv()
            x = cols[s, HEAD:]
            place(cu.at[g], j, jnp.where(left, x, none))
            place(cv.at[g], j, jnp.where(left, none, x))
        onehot(ohc.at[g], [cols.at[g * HALF + j] for j in range(HALF)])

    def quarter(r, g):
        for i in range(3):
            left_rows = rg[r, i * 256 : (i + 1) * 256]
            t = None
            for c in range(3):
                at = slice(c * 256, (c + 1) * 256)
                s = dot_t(left_rows, cu[g, at]) * dot_t(left_rows, cv[g, at])
                hi, lo = split(s)
                mark = ohc[g, :, at]
                step = dot_t(hi, mark) + dot_t(lo, mark)
                t = step if t is None else t + step
            tbuf[i * 256 : (i + 1) * 256] = t
        hi, lo = split(tbuf[...])
        tile[r, :, g * GEX : (g + 1) * GEX] = dot_n(ohr[r], hi) + dot_n(ohr[r], lo)

    take_rows(0)
    take_rows(1)
    take_cols(0)
    quarter(0, 0)
    quarter(1, 0)
    take_cols(1)
    quarter(0, 1)
    swap = pltpu.make_async_remote_copy(
        tile.at[0], sib, sib_s, sib_r, device_id=other, device_id_type=MESH
    )
    swap.start()
    quarter(1, 1)
    swap.wait_recv()
    sends = []
    for j in range(HALF):
        at = slice(j * EX, (j + 1) * EX)
        tile[1, at] = tile[1, at] + sib[at]
        copy = pltpu.make_async_remote_copy(
            tile.at[1, pl.ds(j * EX, EX)], red.at[pair], red_s.at[j], red_r.at[pair],
            device_id=target[j], device_id_type=MESH,
        )
        sends.append(copy)
        if j == 0:

            @pl.when(jnp.logical_not(to_self))
            def _():
                copy.start()

            @pl.when(to_self)
            def _():
                red[pair] = tile[1, at]
        else:
            copy.start()
    for y in range(HALF):

        @pl.when(jnp.logical_not(jnp.logical_and(to_self, pair == y)))
        def _():
            pltpu.make_async_remote_copy(
                tile.at[1, pl.ds(0, EX)], red.at[y], red_s.at[0], red_r.at[y],
                device_id=other, device_id_type=MESH,
            ).wait_recv()

    total = (red[0] + red[1]) + (red[2] + red[3])
    out[...] = pltpu.roll(total, lax.rem(q + SIDE - 1, SIDE) * EX, 1)

    for copy in row_copy + col_copy + [swap] + sends[1:]:
        copy.wait_send()

    @pl.when(jnp.logical_not(to_self))
    def _():
        sends[0].wait_send()


def per_device(acts, out_grads, proj_in, proj_out, segment_ids):
    kin, depth = proj_in.shape[1:]
    kout, width = proj_out.shape[1:]
    layers = lax.axis_size("layer")
    sem = pltpu.SemaphoreType.DMA
    total = pl.pallas_call(
        kernel,
        name="tile",
        out_shape=jax.ShapeDtypeStruct((EX, SIDE * EX), F32),
        in_specs=[pl.BlockSpec(memory_space=pl.ANY)] * 5,
        out_specs=pl.BlockSpec(memory_space=pltpu.VMEM),
        scratch_shapes=[
            pltpu.VMEM((TOK, depth), BF),
            pltpu.VMEM((TOK, width), BF),
            pltpu.VMEM((kin, depth), BF),
            pltpu.VMEM((kout, width), BF),
            pltpu.VMEM((1, TOK), jnp.int32),
            pltpu.VMEM((SIDE, HEAD + TOK, kin + kout), BF),
            pltpu.VMEM((SIDE, HEAD + TOK, kin + kout), BF),
            pltpu.VMEM((2, GTOK, kin + kout), BF),
            pltpu.VMEM((2, GTOK, kin + kout), BF),
            pltpu.VMEM((2, GTOK, kin + kout), BF),
            pltpu.VMEM((2, GEX, GTOK), BF),
            pltpu.VMEM((2, GEX, GTOK), BF),
            pltpu.VMEM((GTOK, GEX), F32),
            pltpu.VMEM((2, GEX, 2 * GEX), F32),
            pltpu.VMEM((GEX, 2 * GEX), F32),
            pltpu.VMEM((HALF, EX, 2 * GEX), F32),
            sem((2 * CHUNKS + 3,)),
            sem((SIDE - 1,)),
            sem((SIDE,)),
            sem((SIDE - 1,)),
            sem((SIDE,)),
            sem,
            sem,
            sem((HALF,)),
            sem((HALF,)),
        ],
        compiler_params=pltpu.CompilerParams(
            collective_id=0, has_side_effects=True, vmem_limit_bytes=60 << 20
        ),
    )(acts, out_grads, proj_in, proj_out, segment_ids)
    return total * (1.0 / (2 * layers * kin * kout))


def solution(mesh):
    in_specs = (
        P("layer", "ex", None),
        P("layer", "ex", None),
        P("layer", None, None),
        P("layer", None, None),
        P("ex", None),
    )
    out_specs = P("ex", "layer")
    return jax.shard_map(
        per_device, mesh=mesh, in_specs=in_specs, out_specs=out_specs, check_vma=False
    )
```

time: 963 us -> 55.7 us (0.06); the launches traced: 949 us -> 55.4 us
  starting transfers between devices: 260 us -> 0 us
  local copies, waits for them, and re-layouts: 218 us -> 0 us
  waiting for transfers between devices: 175 us -> 0 us
  blocking collectives: 136 us -> 0 us
  matrix products: 111 us -> 0 us
  Pallas kernels: 0 us -> 53.8 us
  other arithmetic: 33.8 us -> 1.52 us
  between operations: 13.5 us -> 0.01 us
    ppermute x64 -> x0, starting transfers between devices: 252 us -> none  [from_behind(): return lax.ppermute(block, axis, route)]
    all_gather x1 -> x0, blocking collectives: 136 us -> none  [per_device(): all_labels = lax.all_gather(segment_ids, 'ex', axis=0, tiled=True)]
    dot_general x68 -> x0, matrix products: 111 us -> none  [the longest x32 59.4 us: record(): lax.dot_general(own, visit, (((1,), (1,)), ((), ())), preferred_element_t...]
    convert_element_type x66 -> x0, local copies, waits for them, and re-layouts: 98.2 us -> none  [form_grads(): return built.reshape(count, kout * kin).astype(jnp.bfloat16)]
    reduce_scatter x1 -> x0, waiting for transfers between devices: 98.1 us -> none  [per_device(): lax.psum_scatter(rows_all, 'layer', scatter_dimension=1, tiled=True)]
    while x195 -> x0, local copies, waits for them, and re-layouts: 77.3 us -> none
    ppermute x64 -> x0, waiting for transfers between devices: 66.8 us -> none  [from_behind(): return lax.ppermute(block, axis, route)]
    pallas_call x0 -> x1, Pallas kernels: none -> 53.8 us  [per_device(): pl.pallas_call(kernel, name='tile', out_shape=jax.ShapeDtypeStruct((EX, S...]
  transfers between devices with their start and end apart: 66 -> 0, of which waited for: 34 -> 0; matrix products, arithmetic and copies ran while one was open for 3% -> 0% of each run, Pallas kernels for 0% -> 0%
where the time goes in v1:
time: 55.7 us; the launch traced here: 55.4 us
  Pallas kernels  53.8 us (97%)
  other arithmetic  1.52 us (3%)
    pallas_call x1, Pallas kernels, per_device(): pl.pallas_call(kernel, name='tile', out_shape=jax.ShapeDtypeStruct((EX, S...  53.8 us
    mul x1, other arithmetic, per_device(): return total * (1.0 / (2 * layers * kin * kout))  1.52 us

profile of v1, /device:TPU:1, one launch (start us, length us, event | category | flops | bytes accessed | tf_op | source)
XLA Modules:
  0.0 55.4 jit_solution(10805767912930686612)
XLA Ops:
  0.0 53.8 %tile.1 = f32[48,384]{1,0:T(8,128)} custom-call(bf16[1,192,8192]{2,1,0:T(8,128)(2,1)} %acts.1, bf16[1,192,1024]{2,1,0:T(8,128)(2,1)} %outg.1, bf16[1,64,8192]{2,1,0:T(8,128)(2,1)} %pin.1, bf16[1,64,1024]{2,1,0:T(8,128)(2,1)} %pout.1, s32[1,192]{1,0:T(1,128)} %seg.1), custom_call_target="tpu_custom_call" | custom-call | tf_op jit(solution)/shard_map/tile/pallas_call | solution.py:245
  53.8 1.5 %broadcast_multiply_fusion = f32[48,384]{1,0:T(8,128)} fusion(f32[48,384]{1,0:T(8,128)} %tile.1), kind=kLoop, calls=%fused_computation | loop fusion | flops 18432 | bytes 147456 | tf_op jit(solution)/shard_map/mul | solution.py:282

commit v2 on v1

v2 whole, which is shorter than its diff:
```python
import jax
import jax.numpy as jnp
from jax import lax
from jax.experimental import pallas as pl
from jax.experimental.pallas import tpu as pltpu
from jax.sharding import PartitionSpec as P

MESH = pl.DeviceIdType.MESH
BF = jnp.bfloat16
F32 = jnp.float32

EX = 48
TOK = 192
SIDE = 8
HALF = SIDE // 2
HEAD = 16
GTOK = HALF * TOK
GEX = HALF * EX
CHUNKS = 4


def dot_t(a, b):
    return lax.dot_general(a, b, (((1,), (1,)), ((), ())), preferred_element_type=F32)


def dot_n(a, b):
    return lax.dot_general(a, b, (((1,), (0,)), ((), ())), preferred_element_type=F32)


def split(x):
    hi = x.astype(BF)
    return hi, (x - hi.astype(F32)).astype(BF)


def kernel(
    acts, outg, pin, pout, seg, out,
    ab, gb, pib, pob, segb,
    across, along, rg, cu, cv, ohr, ohc, tbuf, tile, sib, stage, red,
    in_sem, across_s, across_r, along_s, along_r, sib_s, sib_r, red_s, red_r,
):
    layer = lax.axis_index("layer")
    ex = lax.axis_index("ex")
    core = lax.rem(layer, 2)
    pair = layer // 2
    p = ex // SIDE
    q = lax.rem(ex, SIDE)
    kin = pin.shape[1]
    depth = acts.shape[2]
    piece = depth // CHUNKS

    loads = []

    def load(src, dst):
        copy = pltpu.make_async_copy(src, dst, in_sem.at[len(loads)])
        copy.start()
        loads.append(copy)

    for k in range(CHUNKS):
        at = pl.ds(k * piece, piece)
        load(pin.at[0, :, at], pib.at[:, at])
        load(acts.at[0, :, at], ab.at[:, at])
    load(pout.at[0], pob)
    load(outg.at[0], gb)
    load(seg, segb)

    across_peer = [(layer, lax.rem(p + d, SIDE) * SIDE + q) for d in range(1, SIDE)]
    along_peer = [(layer, p * SIDE + lax.rem(q + d, SIDE)) for d in range(1, SIDE)]
    other = (layer + 1 - 2 * core, ex)

    def owner(k, d):
        return (2 * lax.rem(pair + k, HALF) + core, p * SIDE + lax.rem(q + d, SIDE))

    barrier = pltpu.get_barrier_semaphore()
    greet = across_peer + along_peer + [other]
    greet += [owner(k, d) for k in range(1, HALF) for d in range(SIDE)]
    for device in greet:
        pl.semaphore_signal(barrier, inc=1, device_id=device, device_id_type=MESH)

    loads[-1].wait()
    labels = segb[...].astype(F32)
    tail = labels[:, 128:TOK]
    low = labels[:, 0:128]
    line = lax.broadcasted_iota(jnp.int32, (HEAD, 128), 0)
    head = jnp.where(line == 0, low, jnp.concatenate([tail, tail], axis=1)).astype(BF)
    loads[-3].wait()
    loads[-2].wait()
    u = dot_t(gb[...], pob[...])
    v = jnp.zeros((TOK, kin), F32)
    for k in range(CHUNKS):
        loads[2 * k].wait()
        loads[2 * k + 1].wait()
        at = pl.ds(k * piece, piece)
        v = v + dot_t(ab[:, at], pib[:, at])
    own = jnp.concatenate([u, v], axis=1).astype(BF)
    along[1, 0:HEAD] = head
    along[1, HEAD:] = own
    pl.semaphore_wait(barrier, len(greet))

    mine = HALF * (1 - lax.rem(lax.rem(p, 2) + core, 2)) + p // 2
    sent = []
    for d in (1, 7, 2, 6, 3, 5, 4):
        slot = (1 - d) % SIDE
        copy = pltpu.make_async_remote_copy(
            along.at[1], along.at[slot], along_s.at[d - 1], along_r.at[slot],
            device_id=along_peer[d - 1], device_id_type=MESH,
        )
        copy.start()
        sent.append(copy)
        copy = pltpu.make_async_remote_copy(
            along.at[1], across.at[mine], across_s.at[d - 1], across_r.at[mine],
            device_id=across_peer[d - 1], device_id_type=MESH,
        )
        copy.start()
        sent.append(copy)
    across[mine] = along[1]

    def arrived(dst, sem):
        pltpu.make_async_remote_copy(
            dst, dst, sib_s.at[0], sem, device_id=other, device_id_type=MESH
        ).wait_recv()

    lane = lax.broadcasted_iota(jnp.int32, (TOK, 128), 1)
    left = lane < kin
    small = lax.broadcasted_iota(jnp.int32, (1, 128), 1) < TOK - 128
    spot = lax.broadcasted_iota(jnp.int32, (GEX, 128), 0).astype(F32)
    none = jnp.zeros((), BF)

    def place(dst, j, x):
        dst[j * 128 : (j + 1) * 128] = x[0:128]
        dst[HALF * 128 + j * 64 : HALF * 128 + (j + 1) * 64] = x[128:TOK]

    def onehot(dst, blocks):
        heads = [b[0:HEAD].astype(F32) for b in blocks]
        for j in range(HALF):
            mark = heads[j][0:1] + EX * j
            dst[:, j * 128 : (j + 1) * 128] = jnp.where(spot == mark, 1.0, 0.0).astype(BF)
        for m in range(HALF // 2):
            mark = jnp.where(
                small, heads[2 * m][1:2] + EX * 2 * m, heads[2 * m + 1][1:2] + EX * (2 * m + 1)
            )
            at = HALF * 128 + m * 128
            dst[:, at : at + 128] = jnp.where(spot == mark, 1.0, 0.0).astype(BF)

    def take_across(g):
        for s in range(g * HALF, (g + 1) * HALF):

            @pl.when(s != mine)
            def _():
                arrived(across.at[s], across_r.at[s])

        for j in range(HALF):
            x = across[g * HALF + j, HEAD:]
            place(cu.at[g], j, jnp.where(left, x, none))
            place(cv.at[g], j, jnp.where(left, none, x))
        onehot(ohc.at[g], [across.at[g * HALF + j] for j in range(HALF)])

    def take_along(h):
        for s in range(h * HALF, (h + 1) * HALF):
            if s != 1:
                arrived(along.at[s], along_r.at[s])
            place(rg.at[h], s % HALF, along[s, HEAD:])
        onehot(ohr.at[h], [along.at[h * HALF + j] for j in range(HALF)])

    def quarter(g, h):
        for i in range(3):
            left_rows = rg[h, i * 256 : (i + 1) * 256]
            t = None
            for c in range(3):
                at = slice(c * 256, (c + 1) * 256)
                s = dot_t(left_rows, cu[g, at]) * dot_t(left_rows, cv[g, at])
                hi, lo = split(s)
                mark = ohc[g, :, at]
                step = dot_t(hi, mark) + dot_t(lo, mark)
                t = step if t is None else t + step
            tbuf[i * 256 : (i + 1) * 256] = t
        hi, lo = split(tbuf[...])
        tile[g, h] = dot_n(ohr[h], hi) + dot_n(ohr[h], lo)

    def swap(h):
        copy = pltpu.make_async_remote_copy(
            tile.at[0, h], sib.at[h], sib_s.at[h], sib_r.at[h],
            device_id=other, device_id_type=MESH,
        )
        copy.start()
        sent.append(copy)

    def deliver(h):
        arrived(sib.at[h], sib_r.at[h])
        for j in range(HALF):
            s = h * HALF + j
            d = (s - 1) % SIDE
            for x in range(HALF):
                e = x * EX
                rows = slice(j * EX, (j + 1) * EX)
                both = tile[1, h, rows, e : e + EX] + sib[h, rows, e : e + EX]
                stage[s, x, :, 0 : 2 * EX] = jnp.concatenate(
                    [both[0 : EX // 2], both[EX // 2 :]], axis=1
                )
            for k in range(HALF):
                x = lax.rem(pair + k, HALF)
                if k == 0 and d == 0:
                    red[pair, q] = stage[s, x]
                    continue
                copy = pltpu.make_async_remote_copy(
                    stage.at[s, x], red.at[pair, q], red_s.at[s, k], red_r.at[pair, q],
                    device_id=owner(k, d), device_id_type=MESH,
                )
                copy.start()
                sent.append(copy)

    take_across(0)
    take_along(0)
    quarter(0, 0)
    swap(0)
    take_across(1)
    quarter(1, 0)
    deliver(0)
    take_along(1)
    quarter(0, 1)
    swap(1)
    quarter(1, 1)
    deliver(1)

    for d in (0, 7, 1, 6, 2, 5, 3, 4):
        for k in range(HALF):
            if k or d:
                y, z = lax.rem(pair + k, HALF), lax.rem(q + d, SIDE)
                arrived(red.at[y, z], red_r.at[y, z])
    for z in range(SIDE):
        total = (red[0, z] + red[1, z]) + (red[2, z] + red[3, z])
        out[0 : EX // 2, z * EX : (z + 1) * EX] = total[:, 0:EX]
        out[EX // 2 : EX, z * EX : (z + 1) * EX] = total[:, EX : 2 * EX]

    for copy in sent:
        copy.wait_send()


def per_device(acts, out_grads, proj_in, proj_out, segment_ids):
    kin, depth = proj_in.shape[1:]
    kout, width = proj_out.shape[1:]
    layers = lax.axis_size("layer")
    sem = pltpu.SemaphoreType.DMA
    total = pl.pallas_call(
        kernel,
        name="tile",
        out_shape=jax.ShapeDtypeStruct((EX, SIDE * EX), F32),
        in_specs=[pl.BlockSpec(memory_space=pl.ANY)] * 5,
        out_specs=pl.BlockSpec(memory_space=pltpu.VMEM),
        scratch_shapes=[
            pltpu.VMEM((TOK, depth), BF),
            pltpu.VMEM((TOK, width), BF),
            pltpu.VMEM((kin, depth), BF),
            pltpu.VMEM((kout, width), BF),
            pltpu.VMEM((1, TOK), jnp.int32),
            pltpu.VMEM((SIDE, HEAD + TOK, kin + kout), BF),
            pltpu.VMEM((SIDE, HEAD + TOK, kin + kout), BF),
            pltpu.VMEM((2, GTOK, kin + kout), BF),
            pltpu.VMEM((2, GTOK, kin + kout), BF),
            pltpu.VMEM((2, GTOK, kin + kout), BF),
            pltpu.VMEM((2, GEX, GTOK), BF),
            pltpu.VMEM((2, GEX, GTOK), BF),
            pltpu.VMEM((GTOK, GEX), F32),
            pltpu.VMEM((2, 2, GEX, GEX), F32),
            pltpu.VMEM((2, GEX, GEX), F32),
            pltpu.VMEM((SIDE, HALF, EX // 2, 128), F32),
            pltpu.VMEM((HALF, SIDE, EX // 2, 128), F32),
            sem((2 * CHUNKS + 3,)),
            sem((SIDE - 1,)),
            sem((SIDE,)),
            sem((SIDE - 1,)),
            sem((SIDE,)),
            sem((2,)),
            sem((2,)),
            sem((SIDE, HALF)),
            sem((HALF, SIDE)),
        ],
        compiler_params=pltpu.CompilerParams(
            collective_id=0, has_side_effects=True, vmem_limit_bytes=60 << 20
        ),
    )(acts, out_grads, proj_in, proj_out, segment_ids)
    return total * (1.0 / (2 * layers * kin * kout))


def solution(mesh):
    in_specs = (
        P("layer", "ex", None),
        P("layer", "ex", None),
        P("layer", None, None),
        P("layer", None, None),
        P("ex", None),
    )
    out_specs = P("ex", "layer")
    return jax.shard_map(
        per_device, mesh=mesh, in_specs=in_specs, out_specs=out_specs, check_vma=False
    )
```

time: 55.7 us -> 48.5 us (0.87)
  Pallas kernels: 53.8 us -> 46.8 us
    pallas_call x1, Pallas kernels: 53.8 us -> 46.8 us  [per_device(): pl.pallas_call(kernel, name='tile', out_shape=jax.ShapeDtypeStruct((EX, S...]
where the time goes in v2:
time: 48.5 us; the launch traced here: 48.3 us
  Pallas kernels  46.8 us (96%)
  other arithmetic  1.52 us (3%)
    pallas_call x1, Pallas kernels, per_device(): pl.pallas_call(kernel, name='tile', out_shape=jax.ShapeDtypeStruct((EX, S...  46.8 us
    mul x1, other arithmetic, per_device(): return total * (1.0 / (2 * layers * kin * kout))  1.52 us

profile of v2, /device:TPU:1, one launch (start us, length us, event | category | flops | bytes accessed | tf_op | source)
XLA Modules:
  0.0 48.3 jit_solution(3185918799051705290)
XLA Ops:
  0.0 46.8 %tile.1 = f32[48,384]{1,0:T(8,128)} custom-call(bf16[1,192,8192]{2,1,0:T(8,128)(2,1)} %acts.1, bf16[1,192,1024]{2,1,0:T(8,128)(2,1)} %outg.1, bf16[1,64,8192]{2,1,0:T(8,128)(2,1)} %pin.1, bf16[1,64,1024]{2,1,0:T(8,128)(2,1)} %pout.1, s32[1,192]{1,0:T(1,128)} %seg.1), custom_call_target="tpu_custom_call" | custom-call | tf_op jit(solution)/shard_map/tile/pallas_call | solution.py:243
  46.8 1.5 %broadcast_multiply_fusion = f32[48,384]{1,0:T(8,128)} fusion(f32[48,384]{1,0:T(8,128)} %tile.1), kind=kLoop, calls=%fused_computation | loop fusion | flops 18432 | bytes 147456 | tf_op jit(solution)/shard_map/mul | solution.py:281

commit v3 on v2

v3 whole, which is shorter than its diff:
```python
import jax
import jax.numpy as jnp
from jax import lax
from jax.experimental import pallas as pl
from jax.experimental.pallas import tpu as pltpu
from jax.sharding import PartitionSpec as P

MESH = pl.DeviceIdType.MESH
BF = jnp.bfloat16
F32 = jnp.float32

EX = 48
TOK = 192
SIDE = 8
HALF = SIDE // 2
HEAD = 16
GTOK = HALF * TOK
GEX = HALF * EX
UNITS = ((1, 0, 2), (3, 7), (5, 4), (6,))
CODE = 32767.0
CHUNKS = 4


def dot_t(a, b):
    return lax.dot_general(a, b, (((1,), (1,)), ((), ())), preferred_element_type=F32)


def dot_n(a, b):
    return lax.dot_general(a, b, (((1,), (0,)), ((), ())), preferred_element_type=F32)


def split(x):
    hi = x.astype(BF)
    return hi, (x - hi.astype(F32)).astype(BF)


def kernel(
    acts, outg, pin, pout, seg, out,
    ab, gb, pib, pob, segb,
    across, along, cu, cv, ohc, tile, sib, stage, red, acc,
    in_sem, across_s, across_r, along_s, along_r, sib_s, sib_r, red_s, red_r,
):
    layer = lax.axis_index("layer")
    ex = lax.axis_index("ex")
    core = lax.rem(layer, 2)
    pair = layer // 2
    p = ex // SIDE
    q = lax.rem(ex, SIDE)
    kin = pin.shape[1]
    depth = acts.shape[2]
    piece = depth // CHUNKS

    loads = []

    def load(src, dst):
        copy = pltpu.make_async_copy(src, dst, in_sem.at[len(loads)])
        copy.start()
        loads.append(copy)

    for k in range(CHUNKS):
        at = pl.ds(k * piece, piece)
        load(pin.at[0, :, at], pib.at[:, at])
        load(acts.at[0, :, at], ab.at[:, at])
    load(pout.at[0], pob)
    load(outg.at[0], gb)
    load(seg, segb)

    px, py = p // 2, lax.rem(p, 2)

    def across_device(d, e):
        return (layer, (2 * lax.rem(px + d, HALF) + lax.rem(py + e, 2)) * SIDE + q)

    def along_device(d):
        return (layer, p * SIDE + lax.rem(q + d, SIDE))

    other = (layer + 1 - 2 * core, ex)

    def owner(k, d):
        return (2 * lax.rem(pair + k, HALF) + core, p * SIDE + lax.rem(q + d, SIDE))

    barrier = pltpu.get_barrier_semaphore()
    greet = [along_device(d) for d in range(1, SIDE)] + [other]
    greet += [across_device(d, e) for e in range(2) for d in range(HALF) if d or e]
    greet += [owner(k, d) for k in range(1, HALF) for d in range(SIDE)]
    for device in greet:
        pl.semaphore_signal(barrier, inc=1, device_id=device, device_id_type=MESH)

    loads[-1].wait()
    labels = segb[...].astype(F32)
    tail = labels[:, 128:TOK]
    low = labels[:, 0:128]
    line = lax.broadcasted_iota(jnp.int32, (HEAD, 128), 0)
    head = jnp.where(line == 0, low, jnp.concatenate([tail, tail], axis=1)).astype(BF)
    loads[-3].wait()
    loads[-2].wait()
    u = dot_t(gb[...], pob[...])
    v = jnp.zeros((TOK, kin), F32)
    for k in range(CHUNKS):
        loads[2 * k].wait()
        loads[2 * k + 1].wait()
        at = pl.ds(k * piece, piece)
        v = v + dot_t(ab[:, at], pib[:, at])
    own = jnp.concatenate([u, v], axis=1).astype(BF)
    along[1, 0:HEAD] = head
    along[1, HEAD:] = own
    pl.semaphore_wait(barrier, len(greet))

    sent = []

    def send(src, dst, send_sem, recv_sem, device):
        copy = pltpu.make_async_remote_copy(
            src, dst, send_sem, recv_sem, device_id=device, device_id_type=MESH
        )
        copy.start()
        sent.append(copy)

    def send_across(d, e):
        to = HALF * e + px
        sem = across_s.at[HALF * e + d]
        send(along.at[1], across.at[to], sem, across_r.at[to], across_device(d, e))

    def send_along(d):
        to = (1 - d) % SIDE
        send(along.at[1], along.at[to], along_s.at[d], along_r.at[to], along_device(d))

    def pass_on(src, to, d, sem, at):
        rows = pl.ds(*at)
        send(
            along.at[src, rows], along.at[to, rows], along_s.at[sem + SIDE], along_r.at[sem],
            along_device(d),
        )

    for d in (2, 6):
        send_along(d)
    for d in (1, 3, 2):
        send_across(d, 0)
    for d in (1, 7):
        send_along(d)
    for d in (0, 1, 3, 2):
        send_across(d, 1)
    across[px] = along[1]

    def arrived(dst, sem):
        pltpu.make_async_remote_copy(
            dst, dst, sib_s.at[0], sem, device_id=other, device_id_type=MESH
        ).wait_recv()

    lane = lax.broadcasted_iota(jnp.int32, (TOK, 128), 1)
    left = lane < kin
    small = lax.broadcasted_iota(jnp.int32, (1, 128), 1) < TOK - 128
    spot = lax.broadcasted_iota(jnp.int32, (GEX, 128), 0).astype(F32)
    none = jnp.zeros((), BF)
    line48 = lax.broadcasted_iota(jnp.int32, (EX, TOK), 0).astype(F32)

    def place(dst, j, x):
        dst[j * 128 : (j + 1) * 128] = x[0:128]
        dst[HALF * 128 + j * 64 : HALF * 128 + (j + 1) * 64] = x[128:TOK]

    def onehot(dst, blocks):
        heads = [b[0:HEAD].astype(F32) for b in blocks]
        for j in range(HALF):
            mark = heads[j][0:1] + EX * j
            dst[:, j * 128 : (j + 1) * 128] = jnp.where(spot == mark, 1.0, 0.0).astype(BF)
        for m in range(HALF // 2):
            mark = jnp.where(
                small, heads[2 * m][1:2] + EX * 2 * m, heads[2 * m + 1][1:2] + EX * (2 * m + 1)
            )
            at = HALF * 128 + m * 128
            dst[:, at : at + 128] = jnp.where(spot == mark, 1.0, 0.0).astype(BF)

    def take_across(g):
        for d in range(HALF):
            if d or g:
                at = g * HALF + lax.rem(px + d, HALF)
                arrived(across.at[at], across_r.at[at])
        for j in range(HALF):
            x = across[g * HALF + j, HEAD:]
            place(cu.at[g], j, jnp.where(left, x, none))
            place(cv.at[g], j, jnp.where(left, none, x))
        onehot(ohc.at[g], [across.at[g * HALF + j] for j in range(HALF)])

    def take_along(unit):
        for s in unit:
            if s in (0, 2, 4, 6):
                arrived(along.at[s], along_r.at[s])
            elif s == 5:
                arrived(along.at[5, 0 : HEAD + TOK // 2], along_r.at[5])
                arrived(along.at[5, HEAD + TOK // 2 :], along_r.at[8])

    def strip(g, unit):
        left_rows = jnp.concatenate([along[s, HEAD:] for s in unit], axis=0)
        t = None
        for c in range(GTOK // 256):
            at = slice(c * 256, (c + 1) * 256)
            hi, lo = split(dot_t(left_rows, cu[g, at]) * dot_t(left_rows, cv[g, at]))
            mark = ohc[g, :, at]
            step = dot_t(hi, mark) + dot_t(lo, mark)
            t = step if t is None else t + step
        for i, s in enumerate(unit):
            marks = along[s, 0:HEAD].astype(F32)
            mark = jnp.concatenate([marks[0:1], marks[1:2, 0 : TOK - 128]], axis=1)
            mark = jnp.where(line48 == mark, 1.0, 0.0).astype(BF)
            hi, lo = split(t[i * TOK : (i + 1) * TOK])
            tile[g, s] = dot_n(mark, hi) + dot_n(mark, lo)

    keep = lax.rem(py + core, 2)
    give = 1 - keep

    def swap(unit):
        for s in unit:
            send(tile.at[give, s], sib.at[s], sib_s.at[s], sib_r.at[s], other)

    def deliver(unit):
        for s in unit:
            arrived(sib.at[s], sib_r.at[s])
            d = (s - 1) % SIDE
            both = tile[keep, s] + sib[s]
            size = jnp.abs(both)
            top = jnp.max(size, axis=(0, 1), keepdims=True)
            power = jnp.ceil(jnp.log2(jnp.maximum(top, 1e-30)) + 1e-4)
            code = (jnp.sqrt(size * jnp.exp2(-power)) * CODE + 0.5).astype(jnp.int32)
            code = jnp.where(both < 0, -code, code)
            word = code[0 : EX // 2] * 65536 + (code[EX // 2 :] & 65535)
            note = jnp.broadcast_to(power.astype(jnp.int32), (8, 128 - 2 * EX))
            for x in range(HALF):
                w = word[:, x * EX : (x + 1) * EX]
                stage[s, x, 0:8] = jnp.concatenate([w[0:8], w[8:16], note], axis=1)
                stage[s, x, 8:12] = jnp.concatenate([w[16:20], w[20:24], note[0:4]], axis=1)
            to = (1 - d) % SIDE
            for k in range(HALF):
                x = lax.rem(pair + k, HALF)
                if k == 0 and d == 0:
                    red[pair, to] = stage[s, x]
                else:
                    sem = red_r.at[pair, to]
                    send(stage.at[s, x], red.at[pair, to], red_s.at[s, k], sem, owner(k, d))

    arrived(along.at[7], along_r.at[7])
    pass_on(7, 6, 1, 6, (0, HEAD + TOK))
    pass_on(7, 5, 2, 5, (0, HEAD + TOK // 2))
    arrived(along.at[3], along_r.at[3])
    pass_on(3, 4, 7, 4, (0, HEAD + TOK))
    pass_on(3, 5, 6, 8, (HEAD + TOK // 2, TOK // 2))
    take_across(0)
    take_along(UNITS[0])
    strip(0, UNITS[0])
    take_across(1)
    strip(1, UNITS[0])
    swap(UNITS[0])
    for before, unit in zip(UNITS, UNITS[1:]):
        take_along(unit)
        strip(give, unit)
        strip(keep, unit)
        swap(unit)
        deliver(before)
    deliver(UNITS[-1])

    for s in (1, 0, 2, 7, 3, 6, 4, 5):
        sums = []
        for k in range(HALF):
            y = lax.rem(pair + k, HALF)
            if k or s != 1:
                arrived(red.at[y, s], red_r.at[y, s])
        for y in range(HALF):
            word = red[y, s]
            scale = jnp.exp2(word[:, 2 * EX : 2 * EX + 1].astype(F32)) * (1.0 / (CODE * CODE))
            for half in (word >> 16, (word << 16) >> 16):
                code = half.astype(F32)
                sums.append(code * jnp.abs(code) * scale)
        at = slice(s * EX, (s + 1) * EX)
        for h in range(2):
            part = (sums[h] + sums[2 + h]) + (sums[4 + h] + sums[6 + h])
            base = h * (EX // 2)
            acc[base : base + 8, at] = part[0:8, 0:EX]
            acc[base + 8 : base + 16, at] = part[0:8, EX : 2 * EX]
            acc[base + 16 : base + 20, at] = part[8:12, 0:EX]
            acc[base + 20 : base + 24, at] = part[8:12, EX : 2 * EX]
    out[...] = pltpu.roll(acc[...], lax.rem(q + SIDE - 1, SIDE) * EX, 1)

    for copy in sent:
        copy.wait_send()


def per_device(acts, out_grads, proj_in, proj_out, segment_ids):
    kin, depth = proj_in.shape[1:]
    kout, width = proj_out.shape[1:]
    layers = lax.axis_size("layer")
    sem = pltpu.SemaphoreType.DMA
    total = pl.pallas_call(
        kernel,
        name="tile",
        out_shape=jax.ShapeDtypeStruct((EX, SIDE * EX), F32),
        in_specs=[pl.BlockSpec(memory_space=pl.ANY)] * 5,
        out_specs=pl.BlockSpec(memory_space=pltpu.VMEM),
        scratch_shapes=[
            pltpu.VMEM((TOK, depth), BF),
            pltpu.VMEM((TOK, width), BF),
            pltpu.VMEM((kin, depth), BF),
            pltpu.VMEM((kout, width), BF),
            pltpu.VMEM((1, TOK), jnp.int32),
            pltpu.VMEM((SIDE, HEAD + TOK, kin + kout), BF),
            pltpu.VMEM((SIDE, HEAD + TOK, kin + kout), BF),
            pltpu.VMEM((2, GTOK, kin + kout), BF),
            pltpu.VMEM((2, GTOK, kin + kout), BF),
            pltpu.VMEM((2, GEX, GTOK), BF),
            pltpu.VMEM((2, SIDE, EX, GEX), F32),
            pltpu.VMEM((SIDE, EX, GEX), F32),
            pltpu.VMEM((SIDE, HALF, EX // 4, 128), jnp.int32),
            pltpu.VMEM((HALF, SIDE, EX // 4, 128), jnp.int32),
            pltpu.VMEM((EX, SIDE * EX), F32),
            sem((2 * CHUNKS + 3,)),
            sem((SIDE,)),
            sem((SIDE,)),
            sem((2 * SIDE + 1,)),
            sem((SIDE + 1,)),
            sem((SIDE,)),
            sem((SIDE,)),
            sem((SIDE, HALF)),
            sem((HALF, SIDE)),
        ],
        compiler_params=pltpu.CompilerParams(
            collective_id=0, has_side_effects=True, vmem_limit_bytes=60 << 20
        ),
    )(acts, out_grads, proj_in, proj_out, segment_ids)
    return total * (1.0 / (2 * layers * kin * kout))


def solution(mesh):
    in_specs = (
        P("layer", "ex", None),
        P("layer", "ex", None),
        P("layer", None, None),
        P("layer", None, None),
        P("ex", None),
    )
    out_specs = P("ex", "layer")
    return jax.shard_map(
        per_device, mesh=mesh, in_specs=in_specs, out_specs=out_specs, check_vma=False
    )
```

time: 48.5 us -> 45.3 us (0.934)
  Pallas kernels: 46.8 us -> 43.7 us
    pallas_call x1, Pallas kernels: 46.8 us -> 43.7 us  [per_device(): pl.pallas_call(kernel, name='tile', out_shape=jax.ShapeDtypeStruct((EX, S...]
where the time goes in v3:
time: 45.3 us; the launch traced here: 45.2 us
  Pallas kernels  43.7 us (96%)
  other arithmetic  1.52 us (3%)
    pallas_call x1, Pallas kernels, per_device(): pl.pallas_call(kernel, name='tile', out_shape=jax.ShapeDtypeStruct((EX, S...  43.7 us
    mul x1, other arithmetic, per_device(): return total * (1.0 / (2 * layers * kin * kout))  1.52 us

profile of v3, /device:TPU:1, one launch (start us, length us, event | category | flops | bytes accessed | tf_op | source)
XLA Modules:
  0.0 45.2 jit_solution(5933790196229320714)
XLA Ops:
  0.0 43.7 %tile.1 = f32[48,384]{1,0:T(8,128)} custom-call(bf16[1,192,8192]{2,1,0:T(8,128)(2,1)} %acts.1, bf16[1,192,1024]{2,1,0:T(8,128)(2,1)} %outg.1, bf16[1,64,8192]{2,1,0:T(8,128)(2,1)} %pin.1, bf16[1,64,1024]{2,1,0:T(8,128)(2,1)} %pout.1, s32[1,192]{1,0:T(1,128)} %seg.1), custom_call_target="tpu_custom_call" | custom-call | tf_op jit(solution)/shard_map/tile/pallas_call | solution.py:289
  43.7 1.5 %broadcast_multiply_fusion = f32[48,384]{1,0:T(8,128)} fusion(f32[48,384]{1,0:T(8,128)} %tile.1), kind=kLoop, calls=%fused_computation | loop fusion | flops 18432 | bytes 147456 | tf_op jit(solution)/shard_map/mul | solution.py:325

commit v4 on v3

--- a/solution.py
+++ b/solution.py
@@ -16,7 +16,7 @@
 HEAD = 16
 GTOK = HALF * TOK
 GEX = HALF * EX
-UNITS = ((1, 0, 2), (3, 7), (5, 4), (6,))
+UNITS = ((1, 0, 2, 3, 7), (5, 4, 6))
 CODE = 32767.0
 CHUNKS = 4
 
@@ -37,8 +37,8 @@
 def kernel(
     acts, outg, pin, pout, seg, out,
     ab, gb, pib, pob, segb,
-    across, along, cu, cv, ohc, tile, sib, stage, red, acc,
-    in_sem, across_s, across_r, along_s, along_r, sib_s, sib_r, red_s, red_r,
+    across, along, cu, cv, ohc, tile, stage, red, acc,
+    in_sem, across_s, across_r, along_s, along_r, sib_s, sib_r, red_s, red_r, ready,
 ):
     layer = lax.axis_index("layer")
     ex = lax.axis_index("ex")
@@ -57,18 +57,22 @@
         copy.start()
         loads.append(copy)
 
+    load(seg, segb)
+    load(pout.at[0], pob)
+    load(outg.at[0], gb)
     for k in range(CHUNKS):
         at = pl.ds(k * piece, piece)
         load(pin.at[0, :, at], pib.at[:, at])
         load(acts.at[0, :, at], ab.at[:, at])
-    load(pout.at[0], pob)
-    load(outg.at[0], gb)
-    load(seg, segb)
 
     px, py = p // 2, lax.rem(p, 2)
-
-    def across_device(d, e):
-        return (layer, (2 * lax.rem(px + d, HALF) + lax.rem(py + e, 2)) * SIDE + q)
+    home = py == core
+
+    def across_to(d, e):
+        return (2 * pair + py, (2 * lax.rem(px + d, HALF) + lax.rem(py + e, 2)) * SIDE + q)
+
+    def across_from(d, e):
+        return (2 * pair + lax.rem(core + e, 2), (2 * lax.rem(px + d, HALF) + core) * SIDE + q)
 
     def along_device(d):
         return (layer, p * SIDE + lax.rem(q + d, SIDE))
@@ -79,31 +83,46 @@
         return (2 * lax.rem(pair + k, HALF) + core, p * SIDE + lax.rem(q + d, SIDE))
 
     barrier = pltpu.get_barrier_semaphore()
-    greet = [along_device(d) for d in range(1, SIDE)] + [other]
-    greet += [across_device(d, e) for e in range(2) for d in range(HALF) if d or e]
-    greet += [owner(k, d) for k in range(1, HALF) for d in range(SIDE)]
-    for device in greet:
+    def signal(device):
         pl.semaphore_signal(barrier, inc=1, device_id=device, device_id_type=MESH)
 
-    loads[-1].wait()
+    for d in range(1, SIDE):
+        signal(along_device(d))
+    signal(other)
+    for e in range(2):
+        for d in range(HALF):
+            if d or e:
+                signal(across_from(d, e))
+
+    @pl.when(jnp.logical_not(home))
+    def _():
+        signal(across_from(0, 0))
+
+    for k in range(1, HALF):
+        signal(owner(k, 0))
+    greeted = (SIDE - 1) + 1 + SIDE + (HALF - 1) - home.astype(jnp.int32)
+
+    loads[0].wait()
     labels = segb[...].astype(F32)
     tail = labels[:, 128:TOK]
     low = labels[:, 0:128]
     line = lax.broadcasted_iota(jnp.int32, (HEAD, 128), 0)
     head = jnp.where(line == 0, low, jnp.concatenate([tail, tail], axis=1)).astype(BF)
-    loads[-3].wait()
-    loads[-2].wait()
+    loads[1].wait()
+    loads[2].wait()
+    along[0, 1, 0:HEAD] = head
     u = dot_t(gb[...], pob[...])
     v = jnp.zeros((TOK, kin), F32)
     for k in range(CHUNKS):
-        loads[2 * k].wait()
-        loads[2 * k + 1].wait()
+        loads[3 + 2 * k].wait()
+        loads[4 + 2 * k].wait()
         at = pl.ds(k * piece, piece)
         v = v + dot_t(ab[:, at], pib[:, at])
     own = jnp.concatenate([u, v], axis=1).astype(BF)
-    along[1, 0:HEAD] = head
-    along[1, HEAD:] = own
-    pl.semaphore_wait(barrier, len(greet))
+    along[0, 1, HEAD:] = own
+    pl.semaphore_wait(barrier, greeted)
+    for k in range(1, HALF):
+        pl.semaphore_signal(ready, inc=1, device_id=owner(k, 0), device_id_type=MESH)
 
     sent = []
 
@@ -114,21 +133,26 @@
         copy.start()
         sent.append(copy)
 
+    mine = along.at[0]
+    to_across = HALF * lax.rem(core + py, 2) + px
+
     def send_across(d, e):
-        to = HALF * e + px
         sem = across_s.at[HALF * e + d]
-        send(along.at[1], across.at[to], sem, across_r.at[to], across_device(d, e))
+        send(mine.at[1], across.at[to_across], sem, across_r.at[to_across], across_to(d, e))
 
     def send_along(d):
         to = (1 - d) % SIDE
-        send(along.at[1], along.at[to], along_s.at[d], along_r.at[to], along_device(d))
+        send(mine.at[1], mine.at[to], along_s.at[d], along_r.at[to], along_device(d))
 
     def pass_on(src, to, d, sem, at):
         rows = pl.ds(*at)
         send(
-            along.at[src, rows], along.at[to, rows], along_s.at[sem + SIDE], along_r.at[sem],
+            mine.at[src, rows], mine.at[to, rows], along_s.at[sem + SIDE], along_r.at[sem],
             along_device(d),
         )
+
+    def share(s):
+        send(mine.at[s], along.at[1, s], sib_s.at[s], sib_r.at[s], other)
 
     for d in (2, 6):
         send_along(d)
@@ -138,7 +162,19 @@
         send_along(d)
     for d in (0, 1, 3, 2):
         send_across(d, 1)
-    across[px] = along[1]
+    share(1)
+    to_core = pltpu.make_async_remote_copy(
+        mine.at[1], across.at[to_across], across_s.at[0], across_r.at[to_across],
+        device_id=other, device_id_type=MESH,
+    )
+
+    @pl.when(home)
+    def _():
+        across[px] = along[0, 1]
+
+    @pl.when(jnp.logical_not(home))
+    def _():
+        to_core.start()
 
     def arrived(dst, sem):
         pltpu.make_async_remote_copy(
@@ -168,53 +204,52 @@
             at = HALF * 128 + m * 128
             dst[:, at : at + 128] = jnp.where(spot == mark, 1.0, 0.0).astype(BF)
 
-    def take_across(g):
-        for d in range(HALF):
-            if d or g:
-                at = g * HALF + lax.rem(px + d, HALF)
-                arrived(across.at[at], across_r.at[at])
-        for j in range(HALF):
-            x = across[g * HALF + j, HEAD:]
-            place(cu.at[g], j, jnp.where(left, x, none))
-            place(cv.at[g], j, jnp.where(left, none, x))
-        onehot(ohc.at[g], [across.at[g * HALF + j] for j in range(HALF)])
-
-    def take_along(unit):
+    def take_across():
+        for e in range(2):
+            for d in range(HALF):
+                at = e * HALF + lax.rem(px + d, HALF)
+                if d or e:
+                    arrived(across.at[at], across_r.at[at])
+                else:
+
+                    @pl.when(jnp.logical_not(home))
+                    def _():
+                        arrived(across.at[at], across_r.at[at])
+
+        for e in range(2):
+            for j in range(HALF):
+                x = across[e * HALF + j, HEAD:]
+                place(cu.at[e], j, jnp.where(left, x, none))
+                place(cv.at[e], j, jnp.where(left, none, x))
+        onehot(ohc, [across.at[j] for j in range(HALF)])
+
+    def take_along(s):
+        arrived(mine.at[s], along_r.at[s])
+        share(s)
+
+    def strip(unit):
         for s in unit:
-            if s in (0, 2, 4, 6):
-                arrived(along.at[s], along_r.at[s])
-            elif s == 5:
-                arrived(along.at[5, 0 : HEAD + TOK // 2], along_r.at[5])
-                arrived(along.at[5, HEAD + TOK // 2 :], along_r.at[8])
-
-    def strip(g, unit):
-        left_rows = jnp.concatenate([along[s, HEAD:] for s in unit], axis=0)
+            arrived(along.at[1, s], sib_r.at[s])
+        rows = [jnp.concatenate([along[e, s, HEAD:] for s in unit], axis=0) for e in range(2)]
         t = None
         for c in range(GTOK // 256):
             at = slice(c * 256, (c + 1) * 256)
-            hi, lo = split(dot_t(left_rows, cu[g, at]) * dot_t(left_rows, cv[g, at]))
-            mark = ohc[g, :, at]
+            pairs = [dot_t(rows[e], cu[e, at]) * dot_t(rows[e], cv[e, at]) for e in range(2)]
+            hi, lo = split(pairs[0] + pairs[1])
+            mark = ohc[:, at]
             step = dot_t(hi, mark) + dot_t(lo, mark)
             t = step if t is None else t + step
         for i, s in enumerate(unit):
-            marks = along[s, 0:HEAD].astype(F32)
+            marks = along[0, s, 0:HEAD].astype(F32)
             mark = jnp.concatenate([marks[0:1], marks[1:2, 0 : TOK - 128]], axis=1)
             mark = jnp.where(line48 == mark, 1.0, 0.0).astype(BF)
             hi, lo = split(t[i * TOK : (i + 1) * TOK])
-            tile[g, s] = dot_n(mark, hi) + dot_n(mark, lo)
-
-    keep = lax.rem(py + core, 2)
-    give = 1 - keep
-
-    def swap(unit):
-        for s in unit:
-            send(tile.at[give, s], sib.at[s], sib_s.at[s], sib_r.at[s], other)
+            tile[s] = dot_n(mark, hi) + dot_n(mark, lo)
 
     def deliver(unit):
         for s in unit:
-            arrived(sib.at[s], sib_r.at[s])
             d = (s - 1) % SIDE
-            both = tile[keep, s] + sib[s]
+            both = tile[s]
             size = jnp.abs(both)
             top = jnp.max(size, axis=(0, 1), keepdims=True)
             power = jnp.ceil(jnp.log2(jnp.maximum(top, 1e-30)) + 1e-4)
@@ -227,7 +262,7 @@
                 stage[s, x, 0:8] = jnp.concatenate([w[0:8], w[8:16], note], axis=1)
                 stage[s, x, 8:12] = jnp.concatenate([w[16:20], w[20:24], note[0:4]], axis=1)
             to = (1 - d) % SIDE
-            for k in range(HALF):
+            for k in (2, 1, 3, 0):
                 x = lax.rem(pair + k, HALF)
                 if k == 0 and d == 0:
                     red[pair, to] = stage[s, x]
@@ -235,27 +270,30 @@
                     sem = red_r.at[pair, to]
                     send(stage.at[s, x], red.at[pair, to], red_s.at[s, k], sem, owner(k, d))
 
-    arrived(along.at[7], along_r.at[7])
+    arrived(mine.at[7], along_r.at[7])
     pass_on(7, 6, 1, 6, (0, HEAD + TOK))
     pass_on(7, 5, 2, 5, (0, HEAD + TOK // 2))
-    arrived(along.at[3], along_r.at[3])
+    share(7)
+    arrived(mine.at[3], along_r.at[3])
     pass_on(3, 4, 7, 4, (0, HEAD + TOK))
     pass_on(3, 5, 6, 8, (HEAD + TOK // 2, TOK // 2))
-    take_across(0)
-    take_along(UNITS[0])
-    strip(0, UNITS[0])
-    take_across(1)
-    strip(1, UNITS[0])
-    swap(UNITS[0])
-    for before, unit in zip(UNITS, UNITS[1:]):
-        take_along(unit)
-        strip(give, unit)
-        strip(keep, unit)
-        swap(unit)
-        deliver(before)
-    deliver(UNITS[-1])
-
-    for s in (1, 0, 2, 7, 3, 6, 4, 5):
+    share(3)
+    take_along(0)
+    take_along(2)
+    take_across()
+    strip(UNITS[0])
+    take_along(4)
+    take_along(6)
+    arrived(mine.at[5, 0 : HEAD + TOK // 2], along_r.at[5])
+    arrived(mine.at[5, HEAD + TOK // 2 :], along_r.at[8])
+    share(5)
+    pl.semaphore_wait(ready, HALF - 1)
+    deliver(UNITS[0])
+    for unit in UNITS[1:]:
+        strip(unit)
+        deliver(unit)
+
+    for s in (1, 2, 0, 7, 3, 5, 6, 4):
         sums = []
         for k in range(HALF):
             y = lax.rem(pair + k, HALF)
@@ -280,6 +318,10 @@
     for copy in sent:
         copy.wait_send()
 
+    @pl.when(jnp.logical_not(home))
+    def _():
+        to_core.wait_send()
+
 
 def per_device(acts, out_grads, proj_in, proj_out, segment_ids):
     kin, depth = proj_in.shape[1:]
@@ -299,11 +341,10 @@
             pltpu.VMEM((kout, width), BF),
             pltpu.VMEM((1, TOK), jnp.int32),
             pltpu.VMEM((SIDE, HEAD + TOK, kin + kout), BF),
-            pltpu.VMEM((SIDE, HEAD + TOK, kin + kout), BF),
+            pltpu.VMEM((2, SIDE, HEAD + TOK, kin + kout), BF),
             pltpu.VMEM((2, GTOK, kin + kout), BF),
             pltpu.VMEM((2, GTOK, kin + kout), BF),
-            pltpu.VMEM((2, GEX, GTOK), BF),
-            pltpu.VMEM((2, SIDE, EX, GEX), F32),
+            pltpu.VMEM((GEX, GTOK), BF),
             pltpu.VMEM((SIDE, EX, GEX), F32),
             pltpu.VMEM((SIDE, HALF, EX // 4, 128), jnp.int32),
             pltpu.VMEM((HALF, SIDE, EX // 4, 128), jnp.int32),
@@ -317,6 +358,7 @@
             sem((SIDE,)),
             sem((SIDE, HALF)),
             sem((HALF, SIDE)),
+            pltpu.SemaphoreType.REGULAR,
         ],
         compiler_params=pltpu.CompilerParams(
             collective_id=0, has_side_effects=True, vmem_limit_bytes=60 << 20

time: 45.3 us -> 40.5 us (0.89)
  Pallas kernels: 43.7 us -> 38.8 us
    pallas_call x1, Pallas kernels: 43.7 us -> 38.8 us  [per_device(): pl.pallas_call(kernel, name='tile', out_shape=jax.ShapeDtypeStruct((EX, S...]
where the time goes in v4:
time: 40.5 us; the launch traced here: 40.4 us
  Pallas kernels  38.8 us (96%)
  other arithmetic  1.52 us (4%)
    pallas_call x1, Pallas kernels, per_device(): pl.pallas_call(kernel, name='tile', out_shape=jax.ShapeDtypeStruct((EX, S...  38.8 us
    mul x1, other arithmetic, per_device(): return total * (1.0 / (2 * layers * kin * kout))  1.52 us

profile of v4, /device:TPU:1, one launch (start us, length us, event | category | flops | bytes accessed | tf_op | source)
XLA Modules:
  0.0 40.4 jit_solution(4695880988068048630)
XLA Ops:
  0.0 38.8 %tile.1 = f32[48,384]{1,0:T(8,128)} custom-call(bf16[1,192,8192]{2,1,0:T(8,128)(2,1)} %acts.1, bf16[1,192,1024]{2,1,0:T(8,128)(2,1)} %outg.1, bf16[1,64,8192]{2,1,0:T(8,128)(2,1)} %pin.1, bf16[1,64,1024]{2,1,0:T(8,128)(2,1)} %pout.1, s32[1,192]{1,0:T(1,128)} %seg.1), custom_call_target="tpu_custom_call" | custom-call | tf_op jit(solution)/shard_map/tile/pallas_call | solution.py:331
  38.8 1.5 %broadcast_multiply_fusion = f32[48,384]{1,0:T(8,128)} fusion(f32[48,384]{1,0:T(8,128)} %tile.1), kind=kLoop, calls=%fused_computation | loop fusion | flops 18432 | bytes 147456 | tf_op jit(solution)/shard_map/mul | solution.py:367

commit v5 on v4

--- a/solution.py
+++ b/solution.py
@@ -154,14 +154,14 @@
     def share(s):
         send(mine.at[s], along.at[1, s], sib_s.at[s], sib_r.at[s], other)
 
+    for d in (2, 1, 3, 0):
+        send_across(d, 1)
     for d in (2, 6):
         send_along(d)
-    for d in (1, 3, 2):
+    for d in (2, 1, 3):
         send_across(d, 0)
     for d in (1, 7):
         send_along(d)
-    for d in (0, 1, 3, 2):
-        send_across(d, 1)
     share(1)
     to_core = pltpu.make_async_remote_copy(
         mine.at[1], across.at[to_across], across_s.at[0], across_r.at[to_across],
@@ -273,10 +273,10 @@
     arrived(mine.at[7], along_r.at[7])
     pass_on(7, 6, 1, 6, (0, HEAD + TOK))
     pass_on(7, 5, 2, 5, (0, HEAD + TOK // 2))
-    share(7)
     arrived(mine.at[3], along_r.at[3])
     pass_on(3, 4, 7, 4, (0, HEAD + TOK))
     pass_on(3, 5, 6, 8, (HEAD + TOK // 2, TOK // 2))
+    share(7)
     share(3)
     take_along(0)
     take_along(2)

time: 40.5 us -> 40.2 us (level)
  no operation moved by 1% of the time
where the time goes in v5:
time: 40.2 us; the launch traced here: 40.1 us
  Pallas kernels  38.6 us (96%)
  other arithmetic  1.52 us (4%)
    pallas_call x1, Pallas kernels, per_device(): pl.pallas_call(kernel, name='tile', out_shape=jax.ShapeDtypeStruct((EX, S...  38.6 us
    mul x1, other arithmetic, per_device(): return total * (1.0 / (2 * layers * kin * kout))  1.52 us

profile of v5, /device:TPU:1, one launch (start us, length us, event | category | flops | bytes accessed | tf_op | source)
XLA Modules:
  0.0 40.1 jit_solution(16352828448388613032)
XLA Ops:
  0.0 38.6 %tile.1 = f32[48,384]{1,0:T(8,128)} custom-call(bf16[1,192,8192]{2,1,0:T(8,128)(2,1)} %acts.1, bf16[1,192,1024]{2,1,0:T(8,128)(2,1)} %outg.1, bf16[1,64,8192]{2,1,0:T(8,128)(2,1)} %pin.1, bf16[1,64,1024]{2,1,0:T(8,128)(2,1)} %pout.1, s32[1,192]{1,0:T(1,128)} %seg.1), custom_call_target="tpu_custom_call" | custom-call | tf_op jit(solution)/shard_map/tile/pallas_call | solution.py:331
  38.6 1.5 %broadcast_multiply_fusion = f32[48,384]{1,0:T(8,128)} fusion(f32[48,384]{1,0:T(8,128)} %tile.1), kind=kLoop, calls=%fused_computation | loop fusion | flops 18432 | bytes 147456 | tf_op jit(solution)/shard_map/mul | solution.py:367

commit v6 on v5

--- a/solution.py
+++ b/solution.py
@@ -156,8 +156,12 @@
 
     for d in (2, 1, 3, 0):
         send_across(d, 1)
-    for d in (2, 6):
-        send_along(d)
+    first, rest = (0, HEAD + TOK // 2), (HEAD + TOK // 2, TOK // 2)
+    for at, parts in ((first, ((2, 2, 7), (6, 6, 3))), (rest, ((2, 21, 9), (6, 22, 10)))):
+        for d, sem, got in parts:
+            rows = pl.ds(*at)
+            to = mine.at[(1 - d) % SIDE, rows]
+            send(mine.at[1, rows], to, along_s.at[sem], along_r.at[got], along_device(d))
     for d in (2, 1, 3):
         send_across(d, 0)
     for d in (1, 7):
@@ -270,20 +274,26 @@
                     sem = red_r.at[pair, to]
                     send(stage.at[s, x], red.at[pair, to], red_s.at[s, k], sem, owner(k, d))
 
-    arrived(mine.at[7], along_r.at[7])
-    pass_on(7, 6, 1, 6, (0, HEAD + TOK))
-    pass_on(7, 5, 2, 5, (0, HEAD + TOK // 2))
-    arrived(mine.at[3], along_r.at[3])
-    pass_on(3, 4, 7, 4, (0, HEAD + TOK))
-    pass_on(3, 5, 6, 8, (HEAD + TOK // 2, TOK // 2))
+    arrived(mine.at[7, pl.ds(*first)], along_r.at[7])
+    pass_on(7, 6, 1, 6, first)
+    pass_on(7, 5, 2, 5, first)
+    arrived(mine.at[3, pl.ds(*first)], along_r.at[3])
+    pass_on(3, 4, 7, 4, first)
+    arrived(mine.at[7, pl.ds(*rest)], along_r.at[9])
+    pass_on(7, 6, 1, 11, rest)
+    arrived(mine.at[3, pl.ds(*rest)], along_r.at[10])
+    pass_on(3, 4, 7, 12, rest)
+    pass_on(3, 5, 6, 8, rest)
     share(7)
     share(3)
     take_along(0)
     take_along(2)
     take_across()
     strip(UNITS[0])
-    take_along(4)
-    take_along(6)
+    for s, got in ((4, 12), (6, 11)):
+        arrived(mine.at[s, pl.ds(*first)], along_r.at[s])
+        arrived(mine.at[s, pl.ds(*rest)], along_r.at[got])
+        share(s)
     arrived(mine.at[5, 0 : HEAD + TOK // 2], along_r.at[5])
     arrived(mine.at[5, HEAD + TOK // 2 :], along_r.at[8])
     share(5)
@@ -352,8 +362,8 @@
             sem((2 * CHUNKS + 3,)),
             sem((SIDE,)),
             sem((SIDE,)),
-            sem((2 * SIDE + 1,)),
-            sem((SIDE + 1,)),
+            sem((23,)),
+            sem((13,)),
             sem((SIDE,)),
             sem((SIDE,)),
             sem((SIDE, HALF)),

time: 40.2 us -> 40.4 us (level)
  no operation moved by 1% of the time
where the time goes in v6:
time: 40.4 us; the launch traced here: 40.3 us
  Pallas kernels  38.7 us (96%)
  other arithmetic  1.52 us (4%)
    pallas_call x1, Pallas kernels, per_device(): pl.pallas_call(kernel, name='tile', out_shape=jax.ShapeDtypeStruct((EX, S...  38.7 us
    mul x1, other arithmetic, per_device(): return total * (1.0 / (2 * layers * kin * kout))  1.52 us

profile of v6, /device:TPU:1, one launch (start us, length us, event | category | flops | bytes accessed | tf_op | source)
XLA Modules:
  0.0 40.3 jit_solution(12665249499279885606)
XLA Ops:
  0.0 38.7 %tile.1 = f32[48,384]{1,0:T(8,128)} custom-call(bf16[1,192,8192]{2,1,0:T(8,128)(2,1)} %acts.1, bf16[1,192,1024]{2,1,0:T(8,128)(2,1)} %outg.1, bf16[1,64,8192]{2,1,0:T(8,128)(2,1)} %pin.1, bf16[1,64,1024]{2,1,0:T(8,128)(2,1)} %pout.1, s32[1,192]{1,0:T(1,128)} %seg.1), custom_call_target="tpu_custom_call" | custom-call | tf_op jit(solution)/shard_map/tile/pallas_call | solution.py:341
  38.7 1.5 %broadcast_multiply_fusion = f32[48,384]{1,0:T(8,128)} fusion(f32[48,384]{1,0:T(8,128)} %tile.1), kind=kLoop, calls=%fused_computation | loop fusion | flops 18432 | bytes 147456 | tf_op jit(solution)/shard_map/mul | solution.py:377
